TPU v7x, 128 devices: a whole 4x4x4 slice. The times are simulated.
128 devices in a mesh: cells: 32 (over x, z, core), holes: 4 (over y).
Axes of the slice: x: 4, y: 4, z: 4, core: 2. Of those that a mesh axis runs over, the one named last changes fastest.
Arguments:
- pole_grads: bfloat16 [6144, 3, 8192], P('holes', None, 'cells'), may hold values from -3 to 3
- endpoints: int32 [4096, 2], P('holes'), may hold values from 0 to 6143
- current: int32 [16384], P('holes'), may hold values from 0 to 1023
- potential: int32 [16384], P('holes'), may hold values from 0 to 4095
- live_counts: int32 [4], replicated, may hold values from 1 to 4096, 10240 in all
- cell_weight: float32 [8192], P('cells'), may hold values from 0.3 to 3
- basis: bfloat16 [8192, 256], P('cells'), may hold values from -0.125 to 0.125
Outputs:
- gains: bfloat16 [256, 16384], P('cells', 'holes')
All inputs are finite; a program needn't handle non-finite values.
Results may differ from a plain program's by a relative error of at most 0.011.
Values may be sent and summed in bfloat16 or wider, within the bound.
A program may use at most 128 MiB of HBM per device.

v0:
```python
import jax
import jax.numpy as jnp
from jax import lax
from jax.sharding import PartitionSpec as P


def masked_rows(piece, wanted):
    rows = piece.shape[0]
    inside = (wanted >= 0) & (wanted < rows)
    chosen = jnp.take(piece, jnp.clip(wanted, 0, rows - 1), axis=0).astype(jnp.float32)
    return jnp.where(inside[:, None], chosen, jnp.float32(0.0))


def field_adder(ends, piece):
    return masked_rows(piece, ends[:, 0]) - masked_rows(piece, ends[:, 1])


def spread_far(fields, potential):
    cand_count = potential.shape[0]
    blank = jnp.zeros((cand_count, fields.shape[1]), jnp.bfloat16)
    piece = lax.all_gather(fields, "holes", axis=0, tiled=True)
    rows = piece.shape[0]
    inside = (potential >= 0) & (potential < rows)
    chosen = jnp.take(piece, jnp.clip(potential, 0, rows - 1), axis=0)
    return jnp.where(inside[:, None], chosen, blank)


def on_device(pole_grads, endpoints, current, potential, live_counts, cell_weight, basis):
    pole_count, comps, width = pole_grads.shape
    flat = pole_grads.reshape(pole_count, comps * width)
    cand_count = current.shape[0]
    summed = field_adder(endpoints, lax.all_gather(flat, "holes", axis=0, tiled=True))
    fields = summed.astype(jnp.bfloat16)
    far = spread_far(fields, potential)
    near = jnp.take(fields, current, axis=0)
    product = (near.astype(jnp.float32) * far.astype(jnp.float32)).reshape(cand_count, comps, width)
    sens = (jnp.sum(product, axis=1) * cell_weight[None, :]).astype(jnp.bfloat16)
    proj = lax.dot_general(
        basis, sens, (((0,), (1,)), ((), ())), preferred_element_type=jnp.float32
    )
    limit = lax.dynamic_index_in_dim(live_counts, lax.axis_index("holes"), keepdims=False)
    alive = lax.iota(jnp.int32, cand_count) < limit
    proj = jnp.where(alive[None, :], proj, jnp.float32(0.0))
    total = lax.psum(proj, "cells")
    share = total.shape[0] // lax.axis_size("cells")
    mine = lax.dynamic_slice_in_dim(total, lax.axis_index("cells") * share, share, 0)
    return mine.astype(jnp.bfloat16)


def solution(mesh):
    placed = (
        P("holes", None, "cells"),
        P("holes", None),
        P("holes"),
        P("holes"),
        P(),
        P("cells"),
        P("cells", None),
    )
    return jax.shard_map(
        on_device, mesh=mesh, in_specs=placed, out_specs=P("cells", "holes"), check_vma=False
    )
```

profile of v0, /device:TPU:1, one launch (start us, length us, event | category | flops | bytes accessed | tf_op | source)
XLA Modules:
  0.0 392.6 jit_solution(3705296501220416601)
XLA Ops:
  6.5 0.0 copy-start
  6.5 0.0 all-gather.3.cloned.1.call-start
  6.5 2.9 copy.20
  9.4 0.0 copy-start.4
  9.4 2.4 copy.21
  11.9 0.0 all-gather.3.cloned.1.call-update
  11.9 0.0 all-gather.5.cloned.1.call-start
  11.9 0.0 copy-done.4
  12.1 95.2 %all-gather.3.cloned.1.call-done = bf16[6144,768]{1,0:T(8,128)(2,1)} async-done(((bf16[1536,768]{1,0:T(8,128)(2,1)}), bf16[6144,768]{1,0:T(8,128)(2,1)}) %all-gather.3.cloned.1.call-update) | async-done | bytes 9437200 | tf_op jit(solution)/shard_map/all_gather | solution.py:32
  107.2 9.4 %gather_fusion.2 = bf16[1024,768]{1,0:T(8,128)(2,1)S(1)} fusion(bf16[6144,768]{1,0:T(8,128)(2,1)} %all-gather.3.cloned.1.call-done, s32[1024]{0:T(1024)S(1)} %fusion.4), kind=kCustom, calls=%fused_computation.clone | custom fusion | bytes 3149824 | tf_op jit(solution)/shard_map/jit(_take)/gather | solution.py:10
  116.6 9.4 %gather_fusion.3 = bf16[1024,768]{1,0:T(8,128)(2,1)S(1)} fusion(bf16[6144,768]{1,0:T(8,128)(2,1)} %all-gather.3.cloned.1.call-done, s32[1024]{0:T(1024)S(1)} %fusion.5), kind=kCustom, calls=%fused_computation.1.clone | custom fusion | bytes 3149824 | tf_op jit(solution)/shard_map/jit(_take)/gather | solution.py:10
  126.0 0.0 copy-start.6
  126.0 0.0 copy-start.2
  126.0 0.0 copy-start.3
  126.0 2.4 subtract_convert_fusion
  128.5 0.0 copy-start.1
  128.5 0.0 all-gather.5.cloned.1.call-update
  128.5 0.0 copy-done.6
  128.5 0.6 dynamic_slice.7
  129.1 0.7 iota_compare_fusion
  129.7 0.0 copy-done.2
  129.8 0.0 copy-done.3
  129.8 0.0 copy-done.1
  129.9 17.8 %gather_fusion = bf16[4096,768]{1,0:T(8,128)(2,1)} fusion(bf16[1024,768]{1,0:T(8,128)(2,1)S(1)} %copy-done.1, s32[4096]{0:T(1024)S(1)} %fusion.2), kind=kCustom, calls=%fused_computation.2 | custom fusion | bytes 12599296 | tf_op jit(solution)/shard_map/jit(_take)/gather | solution.py:35
  147.6 8.7 %copy.22 = bf16[4096,768]{0,1:T(8,128)(2,1)} copy(bf16[4096,768]{1,0:T(8,128)(2,1)} %gather_fusion) | data formatting | bytes 12582912 | tf_op jit(solution)/shard_map/jit(_take)/gather | solution.py:35
  156.4 38.9 %all-gather.5.cloned.1.call-done = bf16[4096,768]{1,0:T(8,128)(2,1)} async-done(((bf16[1024,768]{1,0:T(8,128)(2,1)}), bf16[4096,768]{1,0:T(8,128)(2,1)}) %all-gather.5.cloned.1.call-update) | async-done | bytes 6291472 | tf_op jit(solution)/shard_map/all_gather | solution.py:21
  195.3 22.7 %gather_fusion.1 = bf16[4096,768]{1,0:T(8,128)(2,1)} fusion(bf16[4096,768]{1,0:T(8,128)(2,1)} %all-gather.5.cloned.1.call-done, s32[4096]{0:T(1024)S(1)} %fusion.3), kind=kCustom, calls=%fused_computation.3 | custom fusion | bytes 12599296 | tf_op jit(solution)/shard_map/jit(_take)/gather | solution.py:24
  218.0 8.6 %copy.23 = bf16[4096,768]{0,1:T(8,128)(2,1)} copy(bf16[4096,768]{1,0:T(8,128)(2,1)} %gather_fusion.1) | data formatting | bytes 12582912 | tf_op jit(solution)/shard_map/jit(_take)/gather | solution.py:24
  226.5 0.0 copy-start.5
  226.5 8.2 %multiply_reduce_fusion = f32[4096,256]{0,1:T(8,128)S(1)} fusion(bf16[4096,3,256]{0,2,1:T(8,128)(2,1)} %bitcast.10, bf16[4096,3,256]{0,2,1:T(8,128)(2,1)} %bitcast.9, pred[4096]{0:T(1024)(128)(4,1)S(1)} %get-tuple-element.9, pred[4096]{0:T(1024)(128)(4,1)S(1)} %get-tuple-element.8, pred[4096]{0:T(1024)(128)(4,1)S(1)} %compare_and_fusion.2), kind=kLoop, calls=%fused_computation.4 | loop fusion | flops 20971520 | bytes 16789504 | tf_op jit(solution)/shard_map/reduce_sum | solution.py:37
  234.8 0.0 copy-done
  234.8 0.0 copy-done.5
  234.8 2.8 fusion
  237.6 147.5 %all-reduce.1 = bf16[256,4096]{1,0:T(8,128)(2,1)S(1)} all-reduce(f32[256,4096]{1,0:T(8,128)} %fusion), channel_id=1, replica_groups=mesh['cells'=32,'holes'=4] {'cells'}, use_global_device_ids=true, to_apply=%region_1.3 | all-reduce | flops 1048576 | bytes 6291456 | tf_op jit(solution)/shard_map/psum | solution.py:44
  385.1 0.6 dynamic-slice_convert_fusion
  (9 shorter events, 0.1 us)
Async XLA Ops:
  6.5 228.2 %copy-start = (bf16[256,256]{1,0:T(8,128)(2,1)S(1)}, bf16[256,256]{1,0:T(8,128)(2,1)}, u32[]{:S(2)}) copy-start(bf16[256,256]{1,0:T(8,128)(2,1)} %param.15) | copy-start | bytes 393220
  6.5 100.7 %all-gather.3.cloned.1.call-start = ((), (), s32[]{:S(2)}) async-start(), calls=%async_computation | async-start | bytes 11796480 | tf_op jit(solution)/shard_map/all_gather | solution.py:32
  9.4 2.5 copy-start.4
  11.9 183.4 %all-gather.5.cloned.1.call-start = ((), (), s32[]{:S(2)}) async-start(), calls=%async_computation.1 | async-start | bytes 7864320 | tf_op jit(solution)/shard_map/all_gather | solution.py:21
  126.0 2.5 copy-start.6
  126.0 3.7 copy-start.2
  126.0 3.8 copy-start.3
  128.5 1.4 copy-start.1
  226.5 8.2 %copy-start.5 = (f32[256]{0:T(256)S(1)}, f32[256]{0:T(256)}, u32[]{:S(2)}) copy-start(f32[256]{0:T(256)} %param.14) | copy-start | bytes 3076
Sparse Core Ops, SparseCore 0:
  12.0 95.1 all-gather.2
  128.6 66.6 all-gather.4
where the time goes:
time: 398 us; the launch traced here: 393 us
  blocking collectives  148 us (37%)
  waiting for transfers between devices  134 us (34%)
  local copies, waits for them, and re-layouts  83.1 us (21%)
  between operations  13.6 us (3%)
  other arithmetic  11.4 us (3%)
    psum x1, blocking collectives, on_device(): total = lax.psum(proj, 'cells')  148 us
    all_gather x1, waiting for transfers between devices, on_device(): lax.all_gather(flat, 'holes', axis=0, tiled=True)  95.2 us
    all_gather x1, waiting for transfers between devices, spread_far(): piece = lax.all_gather(fields, 'holes', axis=0, tiled=True)  38.9 us
    gather x2, local copies, waits for them, and re-layouts, spread_far(): chosen = jnp.take(piece, jnp.clip(potential, 0, rows - 1), axis=0)  31.2 us
    gather x2, local copies, waits for them, and re-layouts, on_device(): near = jnp.take(fields, current, axis=0)  26.5 us
    gather x2, local copies, waits for them, and re-layouts, masked_rows(): jnp.take(piece, jnp.clip(wanted, 0, rows - 1), axis=0).astype(jnp.float32)  18.7 us
    reduce_sum x1, other arithmetic, on_device(): jnp.sum(product, axis=1) * cell_weight[None, :]  8.23 us
  transfers between devices with their start and end apart: 2, of which 2 were waited for; matrix products, arithmetic and copies ran while one was open for 7% of the time, Pallas kernels for 0%

commit v1 on v0

v1 whole, which is shorter than its diff:
```python
import functools

import jax
import jax.numpy as jnp
from jax import lax
from jax.experimental import pallas as pl
from jax.experimental.pallas import tpu as pltpu
from jax.sharding import PartitionSpec as P

F32, BF16, I32 = jnp.float32, jnp.bfloat16, jnp.int32
MESH = pl.DeviceIdType.MESH

LANES = 128
NY, NX, NZ, CORES = 4, 4, 4, 2
CHIPS = NX * NZ
POLES_G, DIP_G, Q_G, BASIS = 1536, 1024, 4096, 256
PARTS = 4
PIECE = POLES_G // PARTS
ROW = 4
BLOCK = 128
OWN_BLOCKS = 11
OWN_Q = OWN_BLOCKS * BLOCK
SUBS = ((0, 4), (4, 8), (8, 11))
ALL_Q = NY * CORES * OWN_Q
IDX_ROWS = 80


def first_blocks(live):
    starts = [0]
    for g in range(NY - 1):
        starts.append(starts[-1] + (live(g) + (BLOCK - 1)) // BLOCK)
    return starts


def kernel(poles, endp, cur, pot, block_rows, weight, basis, out,
           landed, ptab, dtab, own_idx, all_idx, idx, prod, sent, came, wts, bas, bas_t, part, got,
           pole_send, pole_recv, fwd_send, fwd_recv, own_sem, idx_send, idx_recv, idx_sem,
           small_send, small_recv, sens_send, sens_recv, part_send, part_recv, out_send, out_recv):
    cells, y = lax.axis_index("cells"), lax.axis_index("holes")
    core, chip = lax.rem(cells, CORES), lax.div(cells, CORES)
    x, z = lax.div(chip, NZ), lax.rem(chip, NZ)
    sibling = (chip * CORES + 1 - core, y)

    def on_ring(dy):
        return lax.rem(y + dy, NY)

    def on_plane(dx, dz):
        return lax.rem(x + dx, NX) * NZ + lax.rem(z + dz, NZ)

    deltas = [(dx, dz) for dx in range(NX) for dz in range(NZ) if dx or dz]
    back = [deltas.index(((NX - dx) % NX, (NZ - dz) % NZ)) for dx, dz in deltas]

    barrier = pltpu.get_barrier_semaphore()
    for dc in range(CORES):
        for dy in range(NY):
            if dc or dy:
                pl.semaphore_signal(barrier, inc=1, device_id=(chip * CORES + lax.rem(core + dc, CORES), on_ring(dy)), device_id_type=MESH)
    for dx, dz in deltas:
        pl.semaphore_signal(barrier, inc=1, device_id=(on_plane(dx, dz) * CORES + core, y), device_id_type=MESH)

    own_idx[0:16, :] = endp[...] * ROW
    own_idx[16:48, :] = (cur[...] + y * DIP_G) * ROW
    own_idx[48:80, :] = pot[...] * ROW
    wts[core] = weight[...]
    for h in range(2):
        bas[core * 2 + h] = basis[h * LANES:(h + 1) * LANES, :]

    pl.semaphore_wait(barrier, NY * CORES - 1 + len(deltas))

    idx_copies = []
    for dy in range(1, NY):
        idx_copies.append(pltpu.make_async_remote_copy(
            src_ref=own_idx, dst_ref=all_idx.at[pl.ds(pl.multiple_of(y * IDX_ROWS, 8), IDX_ROWS), :], send_sem=idx_send.at[dy], recv_sem=idx_recv.at[dy],
            device_id=(cells, on_ring(dy)), device_id_type=MESH))
        idx_copies[-1].start()
    all_idx[pl.ds(pl.multiple_of(y * IDX_ROWS, 8), IDX_ROWS), :] = own_idx[...]

    def rows_of(group, piece):
        return pl.ds(pl.multiple_of(group * POLES_G + piece * PIECE, PIECE), PIECE)

    def pole_copy(h, piece):
        dest = core * 2 + h
        dy = lax.rem(y - dest + NY, NY)
        return pltpu.make_async_remote_copy(
            src_ref=poles.at[:, pl.ds(piece * PIECE, PIECE), pl.ds(h * LANES, LANES)],
            dst_ref=landed.at[:, rows_of(y, piece), :],
            send_sem=pole_send.at[h, piece], recv_sem=pole_recv.at[dy, piece // CORES],
            device_id=(chip * CORES + piece % CORES, dest), device_id_type=MESH)

    def own_ends(h):
        return poles.at[:, :, pl.ds(h * LANES, LANES)], landed.at[:, pl.ds(pl.multiple_of(y * POLES_G, POLES_G), POLES_G), :]

    def own_local(h):
        return pltpu.make_async_copy(*own_ends(h), own_sem)

    def own_remote(h):
        src, dst = own_ends(h)
        return pltpu.make_async_remote_copy(src_ref=src, dst_ref=dst, send_sem=fwd_send.at[0, 0], recv_sem=fwd_recv.at[0, 0],
                                            device_id=sibling, device_id_type=MESH)

    for h in range(2):
        @pl.when(core * 2 + h != y)
        def _():
            for piece in range(PARTS):
                pole_copy(h, piece).start()

        @pl.when(core * 2 + h == y)
        def _():
            own_local(h).start()
            own_remote(h).start()

    small = []
    for n, (src, dst) in enumerate(((weight, wts.at[core]), (basis.at[0:LANES, :], bas.at[core * 2]), (basis.at[LANES:2 * LANES, :], bas.at[core * 2 + 1]))):
        small.append(pltpu.make_async_remote_copy(src_ref=src, dst_ref=dst, send_sem=small_send.at[n], recv_sem=small_recv.at[n],
                                                  device_id=sibling, device_id_type=MESH))
        small[-1].start()
    for copy in small:
        copy.wait()
    for dy in range(NY):
        bas_t[:, dy * LANES:(dy + 1) * LANES] = jnp.transpose(bas[on_ring(dy)].astype(F32)).astype(BF16)

    for copy in idx_copies:
        copy.wait()
    to_smem = pltpu.make_async_copy(all_idx, idx, idx_sem)
    to_smem.start()
    to_smem.wait()

    def spread(group, piece):
        at = group * POLES_G + piece * PIECE
        for k in range(3):
            block = landed[k, pl.ds(pl.multiple_of(at, PIECE), PIECE), :].astype(F32)
            ptab[pl.ds(at * ROW + k, PIECE, stride=ROW), :] = block

    def forward(dy, n):
        where = landed.at[:, rows_of(on_ring(dy), n * CORES + core), :]
        return pltpu.make_async_remote_copy(src_ref=where, dst_ref=where, send_sem=fwd_send.at[dy, n], recv_sem=fwd_recv.at[dy, n],
                                            device_id=sibling, device_id_type=MESH)

    for h in range(2):
        @pl.when(core * 2 + h == y)
        def _():
            own_local(h).wait()
            own_remote(h).wait_send()

    @pl.when(lax.div(y, 2) != core)
    def _():
        own_remote(0).wait_recv()
    for piece in range(PARTS):
        spread(y, piece)

    forwards = []
    for n in range(PARTS // CORES):
        for dy in (1, 3, 2):
            where = landed.at[:, rows_of(on_ring(dy), n * CORES + core), :]
            pltpu.make_async_remote_copy(src_ref=where, dst_ref=where, send_sem=fwd_send.at[dy, n], recv_sem=pole_recv.at[dy, n],
                                         device_id=sibling, device_id_type=MESH).wait_recv()
            forwards.append(forward(dy, n))
            forwards[-1].start()
            spread(on_ring(dy), n * CORES + core)
    for n in range(PARTS // CORES):
        for dy in (1, 3, 2):
            where = landed.at[:, rows_of(on_ring(dy), n * CORES + 1 - core), :]
            pltpu.make_async_remote_copy(src_ref=where, dst_ref=where, send_sem=fwd_send.at[dy, n], recv_sem=fwd_recv.at[dy, n],
                                         device_id=sibling, device_id_type=MESH).wait_recv()
            spread(on_ring(dy), n * CORES + 1 - core)

    def dipoles(b, _):
        row = lax.div(b, 8) * IDX_ROWS + lax.rem(b, 8) * 2
        for u in range(BLOCK):
            plus, minus = idx[row, u], idx[row + 1, u]
            field = ptab[pl.ds(plus, ROW), :] - ptab[pl.ds(minus, ROW), :]
            dtab[pl.ds(pl.multiple_of(b * (BLOCK * ROW), BLOCK * ROW) + u * ROW, ROW), :] = field.astype(BF16).astype(F32)
        return 0

    lax.fori_loop(0, NY * DIP_G // BLOCK, dipoles, 0)

    mine = wts[lax.div(y, 2), pl.ds(lax.rem(y, 2), 1), :]

    def candidates(dy, m):
        block = (on_ring(dy) * CORES + core) * OWN_BLOCKS + m
        row = block_rows[block]
        for u in range(BLOCK):
            near, far = idx[row, u], idx[row + 32, u]
            prod[u * ROW:(u + 1) * ROW, :] = (dtab[pl.ds(near, ROW), :]
                                              * dtab[pl.ds(far, ROW), :])
        total = prod[pl.ds(0, BLOCK, stride=ROW), :] + prod[pl.ds(1, BLOCK, stride=ROW), :] + prod[pl.ds(2, BLOCK, stride=ROW), :]
        sent[dy, pl.ds(pl.multiple_of(m * BLOCK, BLOCK), BLOCK), :] = (total * mine).astype(BF16)

    def sens_copy(dy, s):
        lo, hi = SUBS[s]
        where = pl.ds(lo * BLOCK, (hi - lo) * BLOCK)
        return pltpu.make_async_remote_copy(
            src_ref=sent.at[dy, where, :], dst_ref=came.at[NY - dy, where, :],
            send_sem=sens_send.at[s, dy], recv_sem=sens_recv.at[s, NY - dy],
            device_id=(cells, on_ring(dy)), device_id_type=MESH)

    def part_copy(s, d):
        lo, hi = SUBS[s]
        dx, dz = deltas[d]
        there = back[d]
        where = pl.ds(lo * BLOCK, (hi - lo) * BLOCK)
        to = on_plane(dx, dz)
        return pltpu.make_async_remote_copy(
            src_ref=part.at[to, :, where], dst_ref=got.at[there, :, where],
            send_sem=part_send.at[s, d], recv_sem=part_recv.at[s, there],
            device_id=(to * CORES + core, y), device_id_type=MESH)

    def project(s):
        lo, hi = SUBS[s]
        where = slice(lo * BLOCK, hi * BLOCK)
        for dy in range(1, NY):
            sens_copy(NY - dy, s).wait_recv()
        for m in range(lo, hi):
            rows = slice(m * BLOCK, (m + 1) * BLOCK)
            sens = jnp.concatenate([sent[0, rows, :]] + [came[dy, rows, :] for dy in range(1, NY)], axis=1)
            proj = lax.dot_general(bas_t[...], sens, (((1,), (1,)), ((), ())), preferred_element_type=F32)
            part[:, :, rows] = proj.astype(BF16).reshape(CHIPS, BASIS // CHIPS, BLOCK)
        for d in range(len(deltas)):
            part_copy(s, d).start()

    for s, (lo, hi) in enumerate(SUBS):
        for dy in (1, 2, 3, 0):
            def step(m, _):
                candidates(dy, m)
                return 0
            lax.fori_loop(lo, hi, step, 0)
            if dy:
                sens_copy(dy, s).start()
        if s:
            project(s - 1)
    project(len(SUBS) - 1)

    here = pl.multiple_of((y * CORES + core) * OWN_Q, LANES)
    for s, (lo, hi) in enumerate(SUBS):
        where = slice(lo * BLOCK, hi * BLOCK)
        total = part[chip, :, where].astype(F32)
        for d in range(len(deltas)):
            part_copy(s, back[d]).wait_recv()
            total = total + got[d, :, where].astype(F32)
        out[:, pl.ds(pl.multiple_of(here + lo * BLOCK, LANES), (hi - lo) * BLOCK)] = total.astype(BF16)

    def out_copy(n, dc, dy):
        where = out.at[:, pl.ds(here, OWN_Q)]
        return pltpu.make_async_remote_copy(
            src_ref=where, dst_ref=where, send_sem=out_send.at[n], recv_sem=out_recv.at[dc, (NY - dy) % NY],
            device_id=(chip * CORES + lax.rem(core + dc, CORES), on_ring(dy)), device_id_type=MESH)

    outs = [out_copy(n, dc, dy) for n, (dc, dy) in enumerate((dc, dy) for dc in range(CORES) for dy in range(NY) if dc or dy)]
    for copy in outs:
        copy.start()

    for s in range(len(SUBS)):
        for dy in range(1, NY):
            sens_copy(dy, s).wait_send()
        for d in range(len(deltas)):
            part_copy(s, d).wait_send()
    for copy in forwards:
        copy.wait_send()
    for h in range(2):
        @pl.when(core * 2 + h != y)
        def _():
            for piece in range(PARTS):
                pole_copy(h, piece).wait_send()
    for copy in outs:
        copy.wait()


def on_device(pole_grads, endpoints, current, potential, live_counts, cell_weight, basis):
    poles = jnp.transpose(pole_grads, (1, 0, 2))
    endp = endpoints.T.reshape(2, DIP_G // LANES, LANES).transpose(1, 0, 2).reshape(2 * DIP_G // LANES, LANES)
    weight = jnp.pad(cell_weight.reshape(2, LANES), ((0, 6), (0, 0)))
    starts = jnp.stack([jnp.int32(s) for s in first_blocks(lambda g: live_counts[g])])
    blocks = lax.iota(I32, ALL_Q // BLOCK)
    group = jnp.sum((blocks[:, None] >= starts[None, 1:]).astype(I32), axis=1)
    first = jnp.max(jnp.where(blocks[:, None] >= starts[None, :], starts[None, :], 0), axis=1)
    block_rows = group * IDX_ROWS + 16 + jnp.minimum(blocks - first, Q_G // BLOCK - 1)
    vmem, dma = pltpu.VMEM, pltpu.SemaphoreType.DMA
    packed = pl.pallas_call(
        kernel,
        out_shape=jax.ShapeDtypeStruct((BASIS // CHIPS, ALL_Q + Q_G), BF16),
        in_specs=[pl.BlockSpec(memory_space=pl.ANY)] + [pl.BlockSpec(memory_space=vmem)] * 3
        + [pl.BlockSpec(memory_space=pltpu.SMEM)] + [pl.BlockSpec(memory_space=vmem)] * 2,
        out_specs=pl.BlockSpec(memory_space=vmem),
        scratch_shapes=[
            vmem((3, NY * POLES_G, LANES), BF16),
            vmem((NY * POLES_G * ROW, LANES), F32),
            vmem((NY * DIP_G * ROW, LANES), F32),
            vmem((IDX_ROWS, LANES), I32),
            vmem((NY * IDX_ROWS, LANES), I32),
            pltpu.SMEM((NY * IDX_ROWS, LANES), I32),
            vmem((BLOCK * ROW, LANES), F32),
            vmem((NY, OWN_Q, LANES), BF16),
            vmem((NY, OWN_Q, LANES), BF16),
            vmem((CORES, 8, LANES), F32),
            vmem((NY, LANES, BASIS), BF16),
            vmem((BASIS, NY * LANES), BF16),
            vmem((CHIPS, BASIS // CHIPS, OWN_Q), BF16),
            vmem((CHIPS - 1, BASIS // CHIPS, OWN_Q), BF16),
            dma((2, PARTS)), dma((NY, PARTS // CORES)), dma((NY, PARTS // CORES)), dma((NY, PARTS // CORES)), dma,
            dma((NY,)), dma((NY,)), dma,
            dma((3,)), dma((3,)),
            dma((len(SUBS), NY)), dma((len(SUBS), NY)),
            dma((len(SUBS), CHIPS - 1)), dma((len(SUBS), CHIPS - 1)),
            dma((NY * CORES - 1,)), dma((CORES, NY)),
        ],
        compiler_params=pltpu.CompilerParams(collective_id=0, has_side_effects=True, vmem_limit_bytes=48 * 2**20),
    )(poles, endp, current.reshape(Q_G // LANES, LANES), potential.reshape(Q_G // LANES, LANES), block_rows, weight, basis)

    group = lax.axis_index("holes")
    first = lax.dynamic_index_in_dim(starts, group, keepdims=False) * BLOCK
    limit = lax.dynamic_index_in_dim(live_counts, group, keepdims=False)
    rows = lax.rem(lax.axis_index("cells"), CORES) * 8
    gains = lax.dynamic_slice(packed, (rows, first), (8, Q_G))
    alive = lax.iota(I32, Q_G) < limit
    return jnp.where(alive[None, :], gains, jnp.zeros((), BF16))


def solution(mesh):
    placed = (
        P("holes", None, "cells"),
        P("holes", None),
        P("holes"),
        P("holes"),
        P(),
        P("cells"),
        P("cells", None),
    )
    return jax.shard_map(
        on_device, mesh=mesh, in_specs=placed, out_specs=P("cells", "holes"), check_vma=False
    )
```

time: 398 us -> 89.6 us (0.23); the launches traced: 393 us -> 89.2 us
  blocking collectives: 148 us -> 0 us
  waiting for transfers between devices: 134 us -> 0 us
  Pallas kernels: 0 us -> 77.5 us
  local copies, waits for them, and re-layouts: 83.1 us -> 7.45 us
  between operations: 13.6 us -> 2.54 us
  other arithmetic: 11.4 us -> 1.65 us
    psum x1 -> x0, blocking collectives: 148 us -> none  [on_device(): total = lax.psum(proj, 'cells')]
    all_gather x2 -> x0, waiting for transfers between devices: 134 us -> none  [the longest x1 95.2 us: on_device(): lax.all_gather(flat, 'holes', axis=0, tiled=True)]
    pallas_call x0 -> x1, Pallas kernels: none -> 77.5 us  [on_device(): pl.pallas_call(kernel, out_shape=jax.ShapeDtypeStruct((BASIS // CHIPS, AL...]
    gather x6 -> x0, local copies, waits for them, and re-layouts: 76.5 us -> none  [the longest x2 31.2 us: spread_far(): chosen = jnp.take(piece, jnp.clip(potential, 0, rows - 1), axis=0)]
    reduce_sum x1, other arithmetic: 8.23 us -> 0.09 us  [on_device(): group = jnp.sum((blocks[:, None] >= starts[None, 1:]).astype(I32), axis=1)]
  transfers between devices with their start and end apart: 2 -> 0, of which waited for: 2 -> 0; matrix products, arithmetic and copies ran while one was open for 7% -> 0% of each run, Pallas kernels for 0% -> 0%
where the time goes in v1:
time: 89.6 us; the launch traced here: 89.2 us
  Pallas kernels  77.5 us (86%)
  local copies, waits for them, and re-layouts  7.45 us (8%)
  between operations  2.54 us (3%)
  other arithmetic  1.65 us (2%)
    pallas_call x1, Pallas kernels, on_device(): pl.pallas_call(kernel, out_shape=jax.ShapeDtypeStruct((BASIS // CHIPS, AL...  77.5 us
    unnamed x10, local copies, waits for them, and re-layouts  4.7 us

profile of v1, /device:TPU:1, one launch (start us, length us, event | category | flops | bytes accessed | tf_op | source)
XLA Modules:
  0.0 89.2 jit_solution(5511559012802443381)
XLA Ops:
  0.0 1.4 %fusion = (s32[1]{0:T(128)}, s32[1]{0:T(128)}, s32[1]{0:T(128)}, s32[1]{0:T(128)}) fusion(s32[4]{0:T(128)} %param.11, s32[]{:T(128)S(6)} %select_n.30), kind=kLoop, calls=%fused_computation.9 | loop fusion | bytes 36 | tf_op jit(solution)/shard_map/jit(dynamic_index_in_dim)/dynamic_slice | solution.py:311
  3.3 0.1 pad_add_fusion.1
  3.4 0.6 dynamic_slice.11
  4.7 0.1 pad_add_fusion
  4.7 0.1 convert_reduce_fusion
  4.8 0.1 select_reduce_fusion
  4.9 0.7 iota_compare_fusion
  5.6 0.7 pad.4.weight
  6.3 0.0 copy-start
  6.3 1.7 %copy-done = bf16[1536,3,256]{2,0,1:T(8,128)(2,1)S(1)} copy-done((bf16[1536,3,256]{2,0,1:T(8,128)(2,1)S(1)}, bf16[1536,3,256]{2,0,1:T(8,128)(2,1)}, u32[]{:S(2)}) %copy-start) | copy-done | bytes 2359320
  7.9 0.0 copy-start.1
  7.9 0.9 %copy-done.1 = bf16[256,256]{1,0:T(8,128)(2,1)S(1)} copy-done((bf16[256,256]{1,0:T(8,128)(2,1)S(1)}, bf16[256,256]{1,0:T(8,128)(2,1)}, u32[]{:S(2)}) %copy-start.1) | copy-done | bytes 131096
  8.8 0.0 copy-start.2
  8.8 0.7 copy-done.2
  9.6 0.0 copy-start.3
  9.6 0.7 copy-done.3
  10.3 0.0 copy-start.4
  10.3 0.7 copy-done.4
  11.0 77.5 %shard_map.73 = bf16[16,15360]{1,0:T(8,128)(2,1)S(1)} custom-call(bf16[3,1536,256]{2,1,0:T(8,128)(2,1)S(1)} %bitcast.19, s32[16,128]{1,0:T(8,128)S(1)} %bitcast.22, s32[32,128]{1,0:T(8,128)S(1)} %bitcast.20, s32[32,128]{1,0:T(8,128)S(1)} %bitcast.21, s32[88]{0:T(128)S(1)} %minimum_add_fusion.block_rows, f32[8,128]{1,0:T(8,128)S(1)} %pad.4.weight, ...), custom_call_target="tpu_custom_call" | custom-call | tf_op jit(solution)/shard_map/pallas_call | solution.py:278
  88.5 0.7 dynamic-slice_select_fusion
  (1 shorter events, 0.0 us)
Async XLA Ops:
  6.3 1.7 %copy-start = (bf16[1536,3,256]{2,0,1:T(8,128)(2,1)S(1)}, bf16[1536,3,256]{2,0,1:T(8,128)(2,1)}, u32[]{:S(2)}) copy-start(bf16[1536,3,256]{2,0,1:T(8,128)(2,1)} %param.7) | copy-start | bytes 7077892
  7.9 0.9 %copy-start.1 = (bf16[256,256]{1,0:T(8,128)(2,1)S(1)}, bf16[256,256]{1,0:T(8,128)(2,1)}, u32[]{:S(2)}) copy-start(bf16[256,256]{1,0:T(8,128)(2,1)} %basis.1) | copy-start | bytes 393220
  8.8 0.7 copy-start.2
  9.6 0.7 copy-start.3
  10.3 0.7 copy-start.4

commit v2 on v1

v2 whole, which is shorter than its diff:
```python
import functools

import jax
import jax.numpy as jnp
from jax import lax
from jax.experimental import pallas as pl
from jax.experimental.pallas import tpu as pltpu
from jax.sharding import PartitionSpec as P

F32, BF16, I32 = jnp.float32, jnp.bfloat16, jnp.int32
MESH = pl.DeviceIdType.MESH

LANES = 128
NY, NX, NZ, CORES = 4, 4, 4, 2
CHIPS = NX * NZ
POLES_G, DIP_G, Q_G, BASIS = 1536, 1024, 4096, 256
PARTS = 8
PIECE = POLES_G // PARTS
ROW = 4
BLOCK = 128
LIVE = 10240
OWN_BLOCKS = LIVE // (NY * CORES * BLOCK)
OWN_Q = OWN_BLOCKS * BLOCK
SUBS = ((0, 4), (4, 8), (8, 10))
IDX_ROWS = 80
Q_ROWS = Q_G // LANES
LIST = 16
MARGIN = 24


def kernel(poles, endp, cur, pot, live, weight, basis, out,
           landed, ptab, dtab, all_idx, lists, idx, prod, sent, came, wts, bas, bas_t, part, got, sums, packed, flat,
           in_sem, pole_send, pole_recv, fwd_send, fwd_recv, own_sem, idx_send, idx_recv, idx_sem,
           small_send, small_recv, sens_send, sens_recv, part_send, part_recv, out_send, out_recv):
    cells, y = lax.axis_index("cells"), lax.axis_index("holes")
    core, chip = lax.rem(cells, CORES), lax.div(cells, CORES)
    x, z = lax.div(chip, NZ), lax.rem(chip, NZ)
    sibling = (chip * CORES + 1 - core, y)

    def on_ring(dy):
        return lax.rem(y + dy, NY)

    def on_plane(dx, dz):
        return lax.rem(x + dx, NX) * NZ + lax.rem(z + dz, NZ)

    deltas = [(dx, dz) for dx in range(NX) for dz in range(NZ) if dx or dz]
    back = [deltas.index(((NX - dx) % NX, (NZ - dz) % NZ)) for dx, dz in deltas]

    barrier = pltpu.get_barrier_semaphore()
    for dc in range(CORES):
        for dy in range(NY):
            if dc or dy:
                pl.semaphore_signal(barrier, inc=1, device_id=(chip * CORES + lax.rem(core + dc, CORES), on_ring(dy)), device_id_type=MESH)
    for dx, dz in deltas:
        pl.semaphore_signal(barrier, inc=1, device_id=(on_plane(dx, dz) * CORES + core, y), device_id_type=MESH)

    def idx_ends(n):
        src, rows, size = ((endp, 0, 16), (cur, 16, 32), (pot, 48, 32))[n]
        return src, all_idx.at[pl.ds(pl.multiple_of(MARGIN + y * IDX_ROWS + rows, 8), size), :]

    small_ends = [(weight, wts.at[core]), (basis.at[0:LANES, :], bas.at[core]), (basis.at[LANES:2 * LANES, :], bas.at[CORES + core])]
    ins = [pltpu.make_async_copy(*ends, in_sem.at[n]) for n, ends in enumerate([idx_ends(0), idx_ends(1), idx_ends(2)] + small_ends)]
    for copy in ins:
        copy.start()

    pl.semaphore_wait(barrier, NY * CORES - 1 + len(deltas))

    idx_copies, small = [], []
    for dy in range(1, NY):
        for n in range(3):
            src, dst = idx_ends(n)
            idx_copies.append(pltpu.make_async_remote_copy(
                src_ref=src, dst_ref=dst, send_sem=idx_send.at[dy, n], recv_sem=idx_recv.at[dy, n],
                device_id=(cells, on_ring(dy)), device_id_type=MESH))
    for n, (src, dst) in enumerate(small_ends):
        small.append(pltpu.make_async_remote_copy(src_ref=src, dst_ref=dst, send_sem=small_send.at[n], recv_sem=small_recv.at[n],
                                                  device_id=sibling, device_id_type=MESH))
    for copy in idx_copies + small:
        copy.start()

    def rows_of(group, piece):
        return pl.ds(pl.multiple_of(group * POLES_G + piece * PIECE, PIECE), PIECE)

    def pole_copy(h, piece):
        dest = h * CORES + core
        dy = lax.rem(y - dest + NY, NY)
        return pltpu.make_async_remote_copy(
            src_ref=poles.at[:, pl.ds(piece * PIECE, PIECE), pl.ds(h * LANES, LANES)],
            dst_ref=landed.at[:, rows_of(y, piece), :],
            send_sem=pole_send.at[h, piece], recv_sem=pole_recv.at[dy, piece // CORES],
            device_id=(chip * CORES + piece % CORES, dest), device_id_type=MESH)

    def own_ends(h):
        return poles.at[:, :, pl.ds(h * LANES, LANES)], landed.at[:, pl.ds(pl.multiple_of(y * POLES_G, POLES_G), POLES_G), :]

    def own_local(h):
        return pltpu.make_async_copy(*own_ends(h), own_sem)

    def own_remote(h):
        src, dst = own_ends(h)
        return pltpu.make_async_remote_copy(src_ref=src, dst_ref=dst, send_sem=fwd_send.at[0, 0], recv_sem=fwd_recv.at[0, 0],
                                            device_id=sibling, device_id_type=MESH)

    for h in range(2):
        @pl.when(h * CORES + core != y)
        def _():
            for piece in range(PARTS):
                pole_copy(h, piece).start()

        @pl.when(h * CORES + core == y)
        def _():
            own_local(h).start()
            own_remote(h).start()

    for copy in ins + small:
        copy.wait()
    for dy in range(NY):
        bas_t[:, dy * LANES:(dy + 1) * LANES] = jnp.transpose(bas[on_ring(dy)].astype(F32)).astype(BF16)
    for copy in idx_copies:
        copy.wait()
    starts = [0]
    for g in range(NY - 1):
        starts.append(starts[-1] + live[g])
    for g in range(NY):
        at = MARGIN + g * IDX_ROWS
        lists[g * 16:(g + 1) * 16, :] = all_idx[at:at + 16, :] * ROW
    lane = lax.broadcasted_iota(I32, (LIST, LANES), 1)
    place = lax.broadcasted_iota(I32, (LIST, LANES), 0) * LANES + lane
    for dy in range(NY):
        row = (on_ring(dy) * CORES + core) * OWN_BLOCKS
        for n, offset in enumerate((16, 48)):
            total = jnp.zeros((LIST, LANES), I32)
            for g in range(NY):
                whole, shift = starts[g] // LANES, starts[g] % LANES
                at = MARGIN + g * IDX_ROWS + offset + jnp.clip(row - whole, -LIST, Q_ROWS)
                same = pltpu.roll(all_idx[pl.ds(at, LIST), :], shift, 1)
                before = pltpu.roll(all_idx[pl.ds(at - 1, LIST), :], shift, 1)
                values = jnp.where(lane >= shift, same, before)
                if n == 0:
                    values = values + g * DIP_G
                since = place + (row * LANES - starts[g])
                total = jnp.where((since >= 0) & (since < live[g]), values, total)
            at = NY * 16 + (dy * 2 + n) * LIST
            lists[at:at + LIST, :] = total * ROW
    to_smem = pltpu.make_async_copy(lists, idx, idx_sem)
    to_smem.start()
    to_smem.wait()

    def spread(group, piece):
        at = group * POLES_G + piece * PIECE
        for k in range(3):
            block = landed[k, pl.ds(pl.multiple_of(at, PIECE), PIECE), :].astype(F32)
            ptab[pl.ds(at * ROW + k, PIECE, stride=ROW), :] = block

    def forward(dy, n):
        where = landed.at[:, rows_of(on_ring(dy), n * CORES + core), :]
        return pltpu.make_async_remote_copy(src_ref=where, dst_ref=where, send_sem=fwd_send.at[dy, n], recv_sem=fwd_recv.at[dy, n],
                                            device_id=sibling, device_id_type=MESH)

    for h in range(2):
        @pl.when(h * CORES + core == y)
        def _():
            own_local(h).wait()
            own_remote(h).wait_send()

    @pl.when(lax.rem(y, CORES) != core)
    def _():
        own_remote(0).wait_recv()
    for piece in range(PARTS):
        spread(y, piece)

    forwards = []
    for n in range(PARTS // CORES):
        for dy in (1, 3, 2):
            where = landed.at[:, rows_of(on_ring(dy), n * CORES + core), :]
            pltpu.make_async_remote_copy(src_ref=where, dst_ref=where, send_sem=fwd_send.at[dy, n], recv_sem=pole_recv.at[dy, n],
                                         device_id=sibling, device_id_type=MESH).wait_recv()
            forwards.append(forward(dy, n))
            forwards[-1].start()
            spread(on_ring(dy), n * CORES + core)
    for n in range(PARTS // CORES):
        for dy in (1, 3, 2):
            where = landed.at[:, rows_of(on_ring(dy), n * CORES + 1 - core), :]
            pltpu.make_async_remote_copy(src_ref=where, dst_ref=where, send_sem=fwd_send.at[dy, n], recv_sem=fwd_recv.at[dy, n],
                                         device_id=sibling, device_id_type=MESH).wait_recv()
            spread(on_ring(dy), n * CORES + 1 - core)

    def dipoles(b, _):
        row = b * 2
        for u in range(BLOCK):
            plus, minus = idx[row, u], idx[row + 1, u]
            field = ptab[pl.ds(plus, ROW), :] - ptab[pl.ds(minus, ROW), :]
            dtab[pl.ds(pl.multiple_of(b * (BLOCK * ROW), BLOCK * ROW) + u * ROW, ROW), :] = field.astype(BF16).astype(F32)
        return 0

    lax.fori_loop(0, NY * DIP_G // BLOCK, dipoles, 0)

    mine = wts[lax.rem(y, CORES), pl.ds(lax.div(y, CORES), 1), :]

    def candidates(dy, m):
        row = NY * 16 + dy * 2 * LIST + m
        for u in range(BLOCK):
            near, far = idx[row, u], idx[row + LIST, u]
            prod[u * ROW:(u + 1) * ROW, :] = (dtab[pl.ds(near, ROW), :]
                                              * dtab[pl.ds(far, ROW), :])
        total = prod[pl.ds(0, BLOCK, stride=ROW), :] + prod[pl.ds(1, BLOCK, stride=ROW), :] + prod[pl.ds(2, BLOCK, stride=ROW), :]
        sent[dy, pl.ds(pl.multiple_of(m * BLOCK, BLOCK), BLOCK), :] = (total * mine).astype(BF16)

    def sens_copy(dy, s):
        lo, hi = SUBS[s]
        where = pl.ds(lo * BLOCK, (hi - lo) * BLOCK)
        return pltpu.make_async_remote_copy(
            src_ref=sent.at[dy, where, :], dst_ref=came.at[NY - dy, where, :],
            send_sem=sens_send.at[s, dy], recv_sem=sens_recv.at[s, NY - dy],
            device_id=(cells, on_ring(dy)), device_id_type=MESH)

    def part_copy(s, d):
        lo, hi = SUBS[s]
        dx, dz = deltas[d]
        there = back[d]
        where = pl.ds(lo * BLOCK, (hi - lo) * BLOCK)
        to = on_plane(dx, dz)
        return pltpu.make_async_remote_copy(
            src_ref=part.at[to, :, where], dst_ref=got.at[there, :, where],
            send_sem=part_send.at[s, d], recv_sem=part_recv.at[s, there],
            device_id=(to * CORES + core, y), device_id_type=MESH)

    def project(s):
        lo, hi = SUBS[s]
        where = slice(lo * BLOCK, hi * BLOCK)
        for dy in range(1, NY):
            sens_copy(NY - dy, s).wait_recv()
        for m in range(lo, hi):
            rows = slice(m * BLOCK, (m + 1) * BLOCK)
            sens = jnp.concatenate([sent[0, rows, :]] + [came[dy, rows, :] for dy in range(1, NY)], axis=1)
            proj = lax.dot_general(bas_t[...], sens, (((1,), (1,)), ((), ())), preferred_element_type=F32)
            part[:, :, rows] = proj.astype(BF16).reshape(CHIPS, BASIS // CHIPS, BLOCK)
        for d in range(len(deltas)):
            part_copy(s, d).start()

    peers = [(dc, dy) for dc in range(CORES) for dy in range(NY) if dc or dy]
    here = (y * CORES + core) * (OWN_BLOCKS // 2)

    def out_copy(s, n):
        lo, hi = SUBS[s]
        dc, dy = peers[n]
        to = lax.rem(core + dc, CORES)
        return pltpu.make_async_remote_copy(
            src_ref=sums.at[to, pl.ds(lo // 2, (hi - lo) // 2)], dst_ref=packed.at[pl.ds(here + lo // 2, (hi - lo) // 2)],
            send_sem=out_send.at[s, n], recv_sem=out_recv.at[s, dc, (NY - dy) % NY],
            device_id=(chip * CORES + to, on_ring(dy)), device_id_type=MESH)

    def add_up(s):
        lo, hi = SUBS[s]
        where = slice(lo * BLOCK, hi * BLOCK)
        total = part[chip, :, where].astype(F32)
        for d in range(len(deltas)):
            part_copy(s, back[d]).wait_recv()
            total = total + got[d, :, where].astype(F32)
        for c in range(CORES):
            for m in range(0, hi - lo, 2):
                pair = [total[c * 8:(c + 1) * 8, k * BLOCK:(k + 1) * BLOCK] for k in (m, m + 1)]
                sums[c, (lo + m) // 2] = jnp.concatenate(pair, axis=0).astype(BF16)
        for n in range(len(peers)):
            out_copy(s, n).start()
        for m in range(lo // 2, hi // 2):
            packed[here + m] = sums[core, m]

    for s, (lo, hi) in enumerate(SUBS):
        for dy in (1, 2, 3, 0):
            def step(m, _):
                candidates(dy, m)
                return 0
            lax.fori_loop(lo, hi, step, 0)
            if dy:
                sens_copy(dy, s).start()
        if s:
            project(s - 1)
    add_up(0)
    project(len(SUBS) - 1)
    for s in range(1, len(SUBS)):
        add_up(s)
    for s in range(len(SUBS)):
        for n in range(len(peers)):
            out_copy(s, n).wait_recv()

    for m in range(LIVE // BLOCK // 2):
        pair = packed[m].astype(F32)
        flat[2 * m] = pair[0:8, :]
        flat[2 * m + 1] = pair[8:16, :]
    first = jnp.int32(0)
    for g in range(1, NY):
        first = jnp.where(y == g, starts[g], first)
    whole, shift, limit = first // LANES, first % LANES, live[y]
    lane = lax.broadcasted_iota(I32, (8, LANES), 1)
    kept = LANES - shift
    turn = lax.rem(kept, LANES)
    turned = pltpu.roll(flat[whole], turn, 1)
    for b in range(Q_ROWS):
        then = pltpu.roll(flat[whole + b + 1], turn, 1)
        value = jnp.where(lane < kept, turned, then)
        out[:, b * LANES:(b + 1) * LANES] = jnp.where(lane + b * LANES < limit, value, 0.0)
        turned = then

    for s in range(len(SUBS)):
        for n in range(len(peers)):
            out_copy(s, n).wait_send()
    for s in range(len(SUBS)):
        for dy in range(1, NY):
            sens_copy(dy, s).wait_send()
        for d in range(len(deltas)):
            part_copy(s, d).wait_send()
    for copy in forwards:
        copy.wait_send()
    for h in range(2):
        @pl.when(h * CORES + core != y)
        def _():
            for piece in range(PARTS):
                pole_copy(h, piece).wait_send()


def on_device(pole_grads, endpoints, current, potential, live_counts, cell_weight, basis):
    poles = jnp.transpose(pole_grads, (1, 0, 2))
    endp = endpoints.T.reshape(2, DIP_G // LANES, LANES).transpose(1, 0, 2).reshape(2 * DIP_G // LANES, LANES)
    weight = cell_weight.reshape(2, LANES)
    vmem, dma = pltpu.VMEM, pltpu.SemaphoreType.DMA
    in_hbm = pl.BlockSpec(memory_space=pltpu.HBM)
    gains = pl.pallas_call(
        kernel,
        out_shape=jax.ShapeDtypeStruct((BASIS // CHIPS // CORES, Q_G), F32),
        in_specs=[in_hbm] * 4 + [pl.BlockSpec(memory_space=pltpu.SMEM)] + [in_hbm] * 2,
        out_specs=pl.BlockSpec(memory_space=vmem),
        scratch_shapes=[
            vmem((3, NY * POLES_G, LANES), BF16),
            vmem((NY * POLES_G * ROW, LANES), F32),
            vmem((NY * DIP_G * ROW, LANES), F32),
            vmem((MARGIN + NY * IDX_ROWS + MARGIN, LANES), I32),
            vmem((NY * (16 + 2 * LIST), LANES), I32),
            pltpu.SMEM((NY * (16 + 2 * LIST), LANES), I32),
            vmem((BLOCK * ROW, LANES), F32),
            vmem((NY, OWN_Q, LANES), BF16),
            vmem((NY, OWN_Q, LANES), BF16),
            vmem((CORES, 2, LANES), F32),
            vmem((NY, LANES, BASIS), BF16),
            vmem((BASIS, NY * LANES), BF16),
            vmem((CHIPS, BASIS // CHIPS, OWN_Q), BF16),
            vmem((CHIPS - 1, BASIS // CHIPS, OWN_Q), BF16),
            vmem((CORES, OWN_BLOCKS // 2, 16, BLOCK), BF16),
            vmem((LIVE // BLOCK // 2, 16, BLOCK), BF16),
            vmem((LIVE // BLOCK + Q_ROWS + 1, 8, BLOCK), F32),
            dma((6,)),
            dma((2, PARTS)), dma((NY, PARTS // CORES)), dma((NY, PARTS // CORES)), dma((NY, PARTS // CORES)), dma,
            dma((NY, 3)), dma((NY, 3)), dma,
            dma((3,)), dma((3,)),
            dma((len(SUBS), NY)), dma((len(SUBS), NY)),
            dma((len(SUBS), CHIPS - 1)), dma((len(SUBS), CHIPS - 1)),
            dma((len(SUBS), NY * CORES - 1)), dma((len(SUBS), CORES, NY)),
        ],
        compiler_params=pltpu.CompilerParams(collective_id=0, has_side_effects=True, vmem_limit_bytes=60 * 2**20),
    )(poles, endp, current.reshape(Q_G // LANES, LANES), potential.reshape(Q_G // LANES, LANES), live_counts, weight, basis)
    return gains.astype(BF16)


def solution(mesh):
    placed = (
        P("holes", None, "cells"),
        P("holes", None),
        P("holes"),
        P("holes"),
        P(),
        P("cells"),
        P("cells", None),
    )
    return jax.shard_map(
        on_device, mesh=mesh, in_specs=placed, out_specs=P("cells", "holes"), check_vma=False
    )
```

time: 89.6 us -> 78.2 us (0.87)
  local copies, waits for them, and re-layouts: 7.45 us -> 0 us
  between operations: 2.54 us -> 0.01 us
  Pallas kernels: 77.5 us -> 76.5 us
    unnamed x10 -> x0, local copies, waits for them, and re-layouts: 4.7 us -> none
    dynamic_slice x2 -> x0, local copies, waits for them, and re-layouts: 2.07 us -> none  [the longest x1 1.45 us: on_device(): limit = lax.dynamic_index_in_dim(live_counts, group, keepdims=False)]
    convert_element_type x0 -> x1, other arithmetic: none -> 1.54 us  [on_device(): return gains.astype(BF16)]
    pallas_call x1, Pallas kernels: 77.5 us -> 76.5 us  [on_device(): pl.pallas_call(kernel, out_shape=jax.ShapeDtypeStruct((BASIS // CHIPS //...]
where the time goes in v2:
time: 78.2 us; the launch traced here: 78 us
  Pallas kernels  76.5 us (98%)
  other arithmetic  1.54 us (2%)
    pallas_call x1, Pallas kernels, on_device(): pl.pallas_call(kernel, out_shape=jax.ShapeDtypeStruct((BASIS // CHIPS //...  76.5 us

profile of v2, /device:TPU:1, one launch (start us, length us, event | category | flops | bytes accessed | tf_op | source)
XLA Modules:
  0.0 78.0 jit_solution(12502731698524926758)
XLA Ops:
  0.0 76.5 %shard_map.73 = f32[8,4096]{1,0:T(8,128)} custom-call(bf16[3,1536,256]{2,1,0:T(8,128)(2,1)} %bitcast.11, s32[16,128]{1,0:T(8,128)} %bitcast.14, s32[32,128]{1,0:T(8,128)} %bitcast.12, s32[32,128]{1,0:T(8,128)} %bitcast.13, s32[4]{0:T(128)} %live.1, f32[2,128]{1,0:T(2,128)} %bitcast.15, bf16[256,256]{1,0:T(8,128)(2,1)} %basis.1), custom_call_target="tpu_custom_call" | custom-call | tf_op jit(solution)/shard_map/pallas_call | solution.py:328
  76.5 1.5 %convert_element_type.3 = bf16[8,4096]{1,0:T(8,128)(2,1)} convert(f32[8,4096]{1,0:T(8,128)} %shard_map.73) | non-fusion elementwise | flops 32768 | bytes 196608 | tf_op jit(solution)/shard_map/convert_element_type | solution.py:361

commit v3 on v2

v3 whole, which is shorter than its diff:
```python
import functools

import jax
import jax.numpy as jnp
from jax import lax
from jax.experimental import pallas as pl
from jax.experimental.pallas import tpu as pltpu
from jax.sharding import PartitionSpec as P

F32, BF16, I32 = jnp.float32, jnp.bfloat16, jnp.int32
MESH = pl.DeviceIdType.MESH

LANES = 128
NY, NX, NZ, CORES = 4, 4, 4, 2
CHIPS = NX * NZ
POLES_G, DIP_G, Q_G, BASIS = 1536, 1024, 4096, 256
PARTS = 8
PIECE = POLES_G // PARTS
ROW = 4
BLOCK = 128
LIVE = 10240
OWN_BLOCKS = LIVE // (NY * CORES * BLOCK)
OWN_Q = OWN_BLOCKS * BLOCK
SUBS = (("x", 0, 2), ("z", 2, 4), ("x", 4, 6), ("z", 6, 8), ("y", 8, 10))
LAG = 3
PLANE = {"y": ("x", "z"), "x": ("y", "z"), "z": ("x", "y")}
IDX_ROWS = 80
Q_ROWS = Q_G // LANES
LIST = 8
MARGIN = 24


def kernel(poles, endp, cur, pot, live, weight, basis, out,
           landed, ptab, dtab, all_idx, lists, idx, prod, sent, came, wts, bas, bas_far, bas_t, part, got, sums, both, packed, flat,
           in_sem, pole_send, pole_recv, fwd_send, fwd_recv, own_sem, idx_send, idx_recv, idx_sem,
           small_send, small_recv, bas_send, bas_recv, sens_send, sens_recv, part_send, part_recv, pair_send, pair_recv, out_send, out_recv, ring_send, ring_recv):
    cells, y = lax.axis_index("cells"), lax.axis_index("holes")
    core, chip = lax.rem(cells, CORES), lax.div(cells, CORES)
    x, z = lax.div(chip, NZ), lax.rem(chip, NZ)
    sibling = (chip * CORES + 1 - core, y)

    def on_ring(dy):
        return lax.rem(y + dy, NY)

    where_am_i = {"x": x, "y": y, "z": z}

    def at(core_there=core, **steps):
        there = {axis: lax.rem(here + steps.get(axis, 0), 4) for axis, here in where_am_i.items()}
        return (there["x"] * NZ + there["z"]) * CORES + core_there, there["y"]

    deltas = [(i, j) for i in range(4) for j in range(4) if i or j]
    back = [deltas.index(((4 - i) % 4, (4 - j) % 4)) for i, j in deltas]

    barrier = pltpu.get_barrier_semaphore()
    greeted = [at(1 - core, y=dy) for dy in range(NY)]
    greeted += [at(x=i, y=j, z=k) for i in range(NX) for j in range(NY) for k in range(NZ) if (i or j or k) and not (i and j and k)]
    for device in greeted:
        pl.semaphore_signal(barrier, inc=1, device_id=device, device_id_type=MESH)

    def idx_ends(n):
        src, rows, size = ((endp, 0, 16), (cur, 16, 32), (pot, 48, 32))[n]
        return src, all_idx.at[pl.ds(pl.multiple_of(MARGIN + y * IDX_ROWS + rows, 8), size), :]

    small_ends = [(weight, wts.at[core]), (basis.at[0:LANES, :], bas.at[core]), (basis.at[LANES:2 * LANES, :], bas.at[CORES + core])]
    ins = [pltpu.make_async_copy(*ends, in_sem.at[n]) for n, ends in enumerate([idx_ends(0), idx_ends(1), idx_ends(2)] + small_ends)]
    for copy in ins:
        copy.start()

    pl.semaphore_wait(barrier, len(greeted))

    idx_copies, small = [], []
    for dy in range(1, NY):
        for n in range(3):
            src, dst = idx_ends(n)
            idx_copies.append(pltpu.make_async_remote_copy(
                src_ref=src, dst_ref=dst, send_sem=idx_send.at[dy, n], recv_sem=idx_recv.at[dy, n],
                device_id=(cells, on_ring(dy)), device_id_type=MESH))
    for n, (src, dst) in enumerate(small_ends):
        small.append(pltpu.make_async_remote_copy(src_ref=src, dst_ref=dst, send_sem=small_send.at[n], recv_sem=small_recv.at[n],
                                                  device_id=sibling, device_id_type=MESH))
    for copy in idx_copies + small:
        copy.start()

    def rows_of(group, piece):
        return pl.ds(pl.multiple_of(group * POLES_G + piece * PIECE, PIECE), PIECE)

    def pole_copy(h, piece):
        dest = h * CORES + core
        dy = lax.rem(y - dest + NY, NY)
        return pltpu.make_async_remote_copy(
            src_ref=poles.at[:, pl.ds(piece * PIECE, PIECE), pl.ds(h * LANES, LANES)],
            dst_ref=landed.at[:, rows_of(y, piece), :],
            send_sem=pole_send.at[h, piece], recv_sem=pole_recv.at[dy, piece // CORES],
            device_id=(chip * CORES + piece % CORES, dest), device_id_type=MESH)

    def own_ends(h):
        return poles.at[:, :, pl.ds(h * LANES, LANES)], landed.at[:, pl.ds(pl.multiple_of(y * POLES_G, POLES_G), POLES_G), :]

    def own_local(h):
        return pltpu.make_async_copy(*own_ends(h), own_sem)

    def own_remote(h):
        src, dst = own_ends(h)
        return pltpu.make_async_remote_copy(src_ref=src, dst_ref=dst, send_sem=fwd_send.at[0, 0], recv_sem=fwd_recv.at[0, 0],
                                            device_id=sibling, device_id_type=MESH)

    for h in range(2):
        @pl.when(h * CORES + core != y)
        def _():
            for piece in range(PARTS):
                pole_copy(h, piece).start()

        @pl.when(h * CORES + core == y)
        def _():
            own_local(h).start()
            own_remote(h).start()

    for copy in ins + small:
        copy.wait()
    far = []
    for n, axis in enumerate("xz"):
        for d in range(1, 4):
            far.append(pltpu.make_async_remote_copy(src_ref=bas.at[y], dst_ref=bas_far.at[n, 4 - d], send_sem=bas_send.at[n, d], recv_sem=bas_recv.at[n, 4 - d],
                                                    device_id=at(**{axis: d}), device_id_type=MESH))
            far[-1].start()
    for copy in idx_copies + far:
        copy.wait()
    for d in range(4):
        columns = slice(d * LANES, (d + 1) * LANES)
        for n, axis in enumerate("yxz"):
            piece = bas[on_ring(d)] if axis == "y" else bas[y] if d == 0 else bas_far[n - 1, d]
            bas_t[n, :, columns] = jnp.transpose(piece.astype(F32)).astype(BF16)
    starts = [0]
    for g in range(NY - 1):
        starts.append(starts[-1] + live[g])
    for g in range(NY):
        first = MARGIN + g * IDX_ROWS
        lists[g * 16:(g + 1) * 16, :] = all_idx[first:first + 16, :] * ROW
    lane = lax.broadcasted_iota(I32, (LIST, LANES), 1)
    place = lax.broadcasted_iota(I32, (LIST, LANES), 0) * LANES + lane
    for s, (axis, lo, hi) in enumerate(SUBS):
        for d in range(4):
            row = lo * NY * CORES + (lax.rem(where_am_i[axis] + d, 4) * CORES + core) * (hi - lo)
            found = []
            for n, offset in enumerate((16, 48)):
                total = jnp.zeros((LIST, LANES), I32)
                for g in range(NY):
                    whole, shift = starts[g] // LANES, starts[g] % LANES
                    window = MARGIN + g * IDX_ROWS + offset + jnp.clip(row - whole, -LIST, Q_ROWS)
                    same = pltpu.roll(all_idx[pl.ds(window, LIST), :], shift, 1)
                    before = pltpu.roll(all_idx[pl.ds(window - 1, LIST), :], shift, 1)
                    values = jnp.where(lane >= shift, same, before)
                    if n == 0:
                        values = values + g * DIP_G
                    since = place + (row * LANES - starts[g])
                    total = jnp.where((since >= 0) & (since < live[g]), values, total)
                found.append(total[0:4, :])
            first = NY * 16 + (s * 4 + d) * LIST
            lists[first:first + LIST, :] = jnp.concatenate(found, axis=0) * ROW
    to_smem = pltpu.make_async_copy(lists, idx.at[pl.ds(0, lists.shape[0])], idx_sem)
    to_smem.start()
    to_smem.wait()

    def spread(group, piece):
        at = group * POLES_G + piece * PIECE
        for k in range(3):
            block = landed[k, pl.ds(pl.multiple_of(at, PIECE), PIECE), :].astype(F32)
            ptab[pl.ds(at * ROW + k, PIECE, stride=ROW), :] = block

    def forward(dy, n):
        where = landed.at[:, rows_of(on_ring(dy), n * CORES + core), :]
        return pltpu.make_async_remote_copy(src_ref=where, dst_ref=where, send_sem=fwd_send.at[dy, n], recv_sem=fwd_recv.at[dy, n],
                                            device_id=sibling, device_id_type=MESH)

    for h in range(2):
        @pl.when(h * CORES + core == y)
        def _():
            own_local(h).wait()
            own_remote(h).wait_send()

    @pl.when(lax.rem(y, CORES) != core)
    def _():
        own_remote(0).wait_recv()
    for piece in range(PARTS):
        spread(y, piece)

    forwards = []
    for n in range(PARTS // CORES):
        for dy in (1, 3, 2):
            where = landed.at[:, rows_of(on_ring(dy), n * CORES + core), :]
            pltpu.make_async_remote_copy(src_ref=where, dst_ref=where, send_sem=fwd_send.at[dy, n], recv_sem=pole_recv.at[dy, n],
                                         device_id=sibling, device_id_type=MESH).wait_recv()
            forwards.append(forward(dy, n))
            forwards[-1].start()
            spread(on_ring(dy), n * CORES + core)
    for n in range(PARTS // CORES):
        for dy in (1, 3, 2):
            where = landed.at[:, rows_of(on_ring(dy), n * CORES + 1 - core), :]
            pltpu.make_async_remote_copy(src_ref=where, dst_ref=where, send_sem=fwd_send.at[dy, n], recv_sem=fwd_recv.at[dy, n],
                                         device_id=sibling, device_id_type=MESH).wait_recv()
            spread(on_ring(dy), n * CORES + 1 - core)

    def column(u, down):
        return idx.at[pl.ds(down, idx.shape[0] - LIST), pl.ds(u, 1)]

    def dipoles(b, _):
        for k in range(2):
            for u in range(BLOCK):
                plus, minus = column(u, 2 * k)[b * 4, 0], column(u, 2 * k + 1)[b * 4, 0]
                spot = (k * BLOCK + u) * ROW
                prod[spot:spot + ROW, :] = ptab[pl.ds(plus, ROW), :] - ptab[pl.ds(minus, ROW), :]
            done = prod[k * BLOCK * ROW:(k + 1) * BLOCK * ROW, :].astype(BF16).astype(F32)
            dtab[pl.ds(pl.multiple_of((b * 2 + k) * (BLOCK * ROW), BLOCK * ROW), BLOCK * ROW), :] = done
        return 0

    lax.fori_loop(0, NY * DIP_G // BLOCK // 2, dipoles, 0)

    mine = wts[lax.rem(y, CORES), pl.ds(lax.div(y, CORES), 1), :]

    def candidates(s, d):
        row = NY * 16 + (s * 4 + d) * LIST
        for k in range(2):
            for u in range(BLOCK):
                near, far = column(u, k)[row, 0], column(u, k + 4)[row, 0]
                spot = (k * BLOCK + u) * ROW
                prod[spot:spot + ROW, :] = dtab[pl.ds(near, ROW), :] * dtab[pl.ds(far, ROW), :]
            one, two, three = (prod[pl.ds(k * BLOCK * ROW + c, BLOCK, stride=ROW), :] for c in range(3))
            sent[d, pl.ds(pl.multiple_of((s * 2 + k) * BLOCK, BLOCK), BLOCK), :] = ((one + two + three) * mine).astype(BF16)

    def sens_copy(s, d):
        axis, lo, hi = SUBS[s]
        where = pl.ds(lo * BLOCK, (hi - lo) * BLOCK)
        return pltpu.make_async_remote_copy(
            src_ref=sent.at[d, where, :], dst_ref=came.at[4 - d, where, :],
            send_sem=sens_send.at[s, d], recv_sem=sens_recv.at[s, 4 - d],
            device_id=at(**{axis: d}), device_id_type=MESH)

    def share(s, i=0, j=0):
        first, second = (where_am_i[axis] for axis in PLANE[SUBS[s][0]])
        return lax.rem(first + i, 4) * 4 + lax.rem(second + j, 4)

    def part_copy(s, d):
        axis, lo, hi = SUBS[s]
        first, second = PLANE[axis]
        i, j = deltas[d]
        where = pl.ds(lo * BLOCK, (hi - lo) * BLOCK)
        return pltpu.make_async_remote_copy(
            src_ref=part.at[share(s, i, j), :, where], dst_ref=got.at[back[d], :, where],
            send_sem=part_send.at[s, d], recv_sem=part_recv.at[s, back[d]],
            device_id=at(**{first: i, second: j}), device_id_type=MESH)

    def project(s):
        axis, lo, hi = SUBS[s]
        for d in range(1, 4):
            sens_copy(s, 4 - d).wait_recv()
        for m in range(lo, hi):
            rows = slice(m * BLOCK, (m + 1) * BLOCK)
            sens = jnp.concatenate([sent[0, rows, :]] + [came[d, rows, :] for d in range(1, 4)], axis=1)
            proj = lax.dot_general(bas_t["yxz".index(axis)], sens, (((1,), (1,)), ((), ())), preferred_element_type=F32)
            part[:, :, rows] = proj.astype(BF16).reshape(CHIPS, BASIS // CHIPS, BLOCK)
        for d in range(len(deltas)):
            part_copy(s, d).start()

    def pair_copy(s):
        _, lo, hi = SUBS[s]
        half = (hi - lo) // 2
        return pltpu.make_async_remote_copy(
            src_ref=sums.at[0, pl.ds(lo // 2, half)], dst_ref=both.at[pl.ds(lo + core * half, half)],
            send_sem=pair_send.at[s], recv_sem=pair_recv.at[s], device_id=sibling, device_id_type=MESH)

    ring = [(dc, dy) for dc in range(CORES) for dy in range(NY) if dc or dy]

    def ring_copy(s, dc, dy):
        _, lo, hi = SUBS[s]
        half = (hi - lo) // 2
        to = lax.rem(core + dc, CORES)
        return pltpu.make_async_remote_copy(
            src_ref=sums.at[to, pl.ds(lo // 2, half)], dst_ref=packed.at[pl.ds(lo * 4 + (y * CORES + core) * half, half)],
            send_sem=ring_send.at[s, dc, dy], recv_sem=ring_recv.at[s, dc, (NY - dy) % NY],
            device_id=(chip * CORES + to, on_ring(dy)), device_id_type=MESH)

    def add_up(s):
        axis, lo, hi = SUBS[s]
        where = slice(lo * BLOCK, hi * BLOCK)
        total = part[share(s), :, where].astype(F32)
        for d in range(len(deltas)):
            part_copy(s, back[d]).wait_recv()
            total = total + got[d, :, where].astype(F32)
        if axis == "y":
            for m in range(0, hi - lo, 2):
                for c in range(CORES):
                    sums[c, (lo + m) // 2] = jnp.concatenate([total[c * 8:(c + 1) * 8, k * BLOCK:(k + 1) * BLOCK] for k in (m, m + 1)], axis=0).astype(BF16)
            for dc, dy in ring:
                ring_copy(s, dc, dy).start()
            first = lo * 4 + (y * CORES + core) * ((hi - lo) // 2)
            for m in range((hi - lo) // 2):
                packed[first + m] = sums[core, lo // 2 + m]
            return
        for m in range(0, hi - lo, 2):
            pairs = [jnp.concatenate([total[c * 8:(c + 1) * 8, k * BLOCK:(k + 1) * BLOCK] for k in (m, m + 1)], axis=0).astype(BF16) for c in range(CORES)]
            kept = jnp.where(core == 0, pairs[0].astype(F32), pairs[1].astype(F32)).astype(BF16)
            sums[0, (lo + m) // 2] = jnp.where(core == 0, pairs[1].astype(F32), pairs[0].astype(F32)).astype(BF16)
            both[lo + core * ((hi - lo) // 2) + m // 2] = kept
        pair_copy(s).start()

    def out_copy(s, dy, source):
        axis, lo, hi = SUBS[s]
        return pltpu.make_async_remote_copy(
            src_ref=both.at[pl.ds(lo, hi - lo)], dst_ref=packed.at[pl.ds(lo * 4 + where_am_i[axis] * (hi - lo), hi - lo)],
            send_sem=out_send.at[s, dy], recv_sem=out_recv.at[s, source],
            device_id=(share(s) * CORES + core, on_ring(dy)), device_id_type=MESH)

    def send_out(s):
        axis, lo, hi = SUBS[s]
        pair_copy(s).wait_recv()
        for dy in range(1, NY):
            out_copy(s, dy, where_am_i[axis]).start()

        @pl.when(share(s) != chip)
        def _():
            out_copy(s, 0, where_am_i[axis]).start()

        @pl.when(share(s) == chip)
        def _():
            for m in range(hi - lo):
                packed[lo * 4 + where_am_i[axis] * (hi - lo) + m] = both[lo + m]

    def steps(n, _):
        part_now, d = lax.div(n, 4), lax.rem(n + 1, 4)
        candidates(part_now, d)
        for s in range(len(SUBS)):
            @pl.when((part_now == s) & (d != 0))
            def _():
                sens_copy(s, d).start()
        for s in range(len(SUBS) - LAG):
            @pl.when((part_now == s + LAG) & (d == 0))
            def _():
                project(s)
        return 0

    lax.fori_loop(0, 4 * len(SUBS), steps, 0)
    for s in range(len(SUBS) - LAG, len(SUBS)):
        project(s)
    hopping = [s for s, (axis, _, _) in enumerate(SUBS) if axis != "y"]
    for s in range(len(SUBS)):
        add_up(s)
        if s - 1 in hopping:
            send_out(s - 1)
    for s, (axis, lo, hi) in enumerate(SUBS):
        if s not in hopping:
            for dc, dy in ring:
                ring_copy(s, dc, dy).wait_recv()
            continue
        for source in range(4):
            @pl.when((share(s) != chip) | (where_am_i[axis] != source))
            def _():
                out_copy(s, 1, source).wait_recv()

    for m in range(LIVE // BLOCK // 2):
        pair = packed[m].astype(F32)
        flat[2 * m] = pair[0:8, :]
        flat[2 * m + 1] = pair[8:16, :]
    first = jnp.int32(0)
    for g in range(1, NY):
        first = jnp.where(y == g, starts[g], first)
    whole, shift, limit = first // LANES, first % LANES, live[y]
    lane = lax.broadcasted_iota(I32, (8, LANES), 1)
    kept = LANES - shift
    turn = lax.rem(kept, LANES)
    turned = pltpu.roll(flat[whole], turn, 1)
    for b in range(Q_ROWS):
        then = pltpu.roll(flat[whole + b + 1], turn, 1)
        value = jnp.where(lane < kept, turned, then)
        out[:, b * LANES:(b + 1) * LANES] = jnp.where(lane + b * LANES < limit, value, 0.0)
        turned = then

    for s in range(len(SUBS)):
        for d in range(1, 4):
            sens_copy(s, d).wait_send()
        for d in range(len(deltas)):
            part_copy(s, d).wait_send()
        if SUBS[s][0] == "y":
            for dc, dy in ring:
                ring_copy(s, dc, dy).wait_send()
            continue
        pair_copy(s).wait_send()
        for dy in range(1, NY):
            out_copy(s, dy, 0).wait_send()

        @pl.when(share(s) != chip)
        def _():
            out_copy(s, 0, 0).wait_send()
    for copy in forwards:
        copy.wait_send()
    for h in range(2):
        @pl.when(h * CORES + core != y)
        def _():
            for piece in range(PARTS):
                pole_copy(h, piece).wait_send()


def on_device(pole_grads, endpoints, current, potential, live_counts, cell_weight, basis):
    poles = jnp.transpose(pole_grads, (1, 0, 2))
    endp = endpoints.T.reshape(2, DIP_G // LANES, LANES).transpose(1, 0, 2).reshape(2 * DIP_G // LANES, LANES)
    weight = cell_weight.reshape(2, LANES)
    vmem, dma = pltpu.VMEM, pltpu.SemaphoreType.DMA
    in_hbm = pl.BlockSpec(memory_space=pltpu.HBM)
    gains = pl.pallas_call(
        kernel,
        out_shape=jax.ShapeDtypeStruct((BASIS // CHIPS // CORES, Q_G), F32),
        in_specs=[in_hbm] * 4 + [pl.BlockSpec(memory_space=pltpu.SMEM)] + [in_hbm] * 2,
        out_specs=pl.BlockSpec(memory_space=vmem),
        scratch_shapes=[
            vmem((3, NY * POLES_G, LANES), BF16),
            vmem((NY * POLES_G * ROW, LANES), F32),
            vmem((NY * DIP_G * ROW, LANES), F32),
            vmem((MARGIN + NY * IDX_ROWS + MARGIN, LANES), I32),
            vmem((NY * 16 + len(SUBS) * 4 * LIST, LANES), I32),
            pltpu.SMEM((NY * 16 + len(SUBS) * 4 * LIST + LIST, LANES), I32),
            vmem((2 * BLOCK * ROW, LANES), F32),
            vmem((NY, OWN_Q, LANES), BF16),
            vmem((NY, OWN_Q, LANES), BF16),
            vmem((CORES, 2, LANES), F32),
            vmem((NY, LANES, BASIS), BF16),
            vmem((2, 4, LANES, BASIS), BF16),
            vmem((3, BASIS, 4 * LANES), BF16),
            vmem((CHIPS, BASIS // CHIPS, OWN_Q), BF16),
            vmem((CHIPS - 1, BASIS // CHIPS, OWN_Q), BF16),
            vmem((CORES, OWN_BLOCKS // 2, 16, BLOCK), BF16),
            vmem((OWN_BLOCKS, 16, BLOCK), BF16),
            vmem((LIVE // BLOCK // 2, 16, BLOCK), BF16),
            vmem((LIVE // BLOCK + Q_ROWS + 1, 8, BLOCK), F32),
            dma((6,)),
            dma((2, PARTS)), dma((NY, PARTS // CORES)), dma((NY, PARTS // CORES)), dma((NY, PARTS // CORES)), dma,
            dma((NY, 3)), dma((NY, 3)), dma,
            dma((3,)), dma((3,)),
            dma((2, 4)), dma((2, 4)),
            dma((len(SUBS), 4)), dma((len(SUBS), 4)),
            dma((len(SUBS), CHIPS - 1)), dma((len(SUBS), CHIPS - 1)),
            dma((len(SUBS),)), dma((len(SUBS),)),
            dma((len(SUBS), NY)), dma((len(SUBS), NY)),
            dma((len(SUBS), CORES, NY)), dma((len(SUBS), CORES, NY)),
        ],
        compiler_params=pltpu.CompilerParams(collective_id=0, has_side_effects=True, vmem_limit_bytes=60 * 2**20),
    )(poles, endp, current.reshape(Q_G // LANES, LANES), potential.reshape(Q_G // LANES, LANES), live_counts, weight, basis)
    return gains.astype(BF16)


def solution(mesh):
    placed = (
        P("holes", None, "cells"),
        P("holes", None),
        P("holes"),
        P("holes"),
        P(),
        P("cells"),
        P("cells", None),
    )
    return jax.shard_map(
        on_device, mesh=mesh, in_specs=placed, out_specs=P("cells", "holes"), check_vma=False
    )
```

time: 78.2 us -> 75.5 us (0.965)
  Pallas kernels: 76.5 us -> 73.8 us
    pallas_call x1, Pallas kernels: 76.5 us -> 73.8 us  [on_device(): pl.pallas_call(kernel, out_shape=jax.ShapeDtypeStruct((BASIS // CHIPS //...]
where the time goes in v3:
time: 75.5 us; the launch traced here: 75.4 us
  Pallas kernels  73.8 us (98%)
  other arithmetic  1.54 us (2%)
    pallas_call x1, Pallas kernels, on_device(): pl.pallas_call(kernel, out_shape=jax.ShapeDtypeStruct((BASIS // CHIPS //...  73.8 us
    convert_element_type x1, other arithmetic, on_device(): return gains.astype(BF16)  1.54 us

profile of v3, /device:TPU:1, one launch (start us, length us, event | category | flops | bytes accessed | tf_op | source)
XLA Modules:
  0.0 75.4 jit_solution(9236332016897268608)
XLA Ops:
  0.0 73.8 %shard_map.73 = f32[8,4096]{1,0:T(8,128)} custom-call(bf16[3,1536,256]{2,1,0:T(8,128)(2,1)} %bitcast.11, s32[16,128]{1,0:T(8,128)} %bitcast.14, s32[32,128]{1,0:T(8,128)} %bitcast.12, s32[32,128]{1,0:T(8,128)} %bitcast.13, s32[4]{0:T(128)} %live.1, f32[2,128]{1,0:T(2,128)} %bitcast.15, bf16[256,256]{1,0:T(8,128)(2,1)} %basis.1), custom_call_target="tpu_custom_call" | custom-call | tf_op jit(solution)/shard_map/pallas_call | solution.py:408
  73.8 1.5 %convert_element_type.3 = bf16[8,4096]{1,0:T(8,128)(2,1)} convert(f32[8,4096]{1,0:T(8,128)} %shard_map.73) | non-fusion elementwise | flops 32768 | bytes 196608 | tf_op jit(solution)/shard_map/convert_element_type | solution.py:446

commit v4 on v3

--- a/solution.py
+++ b/solution.py
@@ -21,17 +21,17 @@
 LIVE = 10240
 OWN_BLOCKS = LIVE // (NY * CORES * BLOCK)
 OWN_Q = OWN_BLOCKS * BLOCK
-SUBS = (("x", 0, 2), ("z", 2, 4), ("x", 4, 6), ("z", 6, 8), ("y", 8, 10))
+SUBS = (("y", 0, 2), ("x", 2, 4), ("z", 4, 6), ("x", 6, 8), ("y", 8, 10))
 LAG = 3
 PLANE = {"y": ("x", "z"), "x": ("y", "z"), "z": ("x", "y")}
 IDX_ROWS = 80
 Q_ROWS = Q_G // LANES
-LIST = 8
-MARGIN = 24
+LIST = LIVE // LANES
+MARGIN = 88
 
 
 def kernel(poles, endp, cur, pot, live, weight, basis, out,
-           landed, ptab, dtab, all_idx, lists, idx, prod, sent, came, wts, bas, bas_far, bas_t, part, got, sums, both, packed, flat,
+           landed, ptab, dtab, all_idx, lists, idx, prod, sent, came, wts, bas, bas_own, bas_t, part, got, sums, both, packed, flat,
            in_sem, pole_send, pole_recv, fwd_send, fwd_recv, own_sem, idx_send, idx_recv, idx_sem,
            small_send, small_recv, bas_send, bas_recv, sens_send, sens_recv, part_send, part_recv, pair_send, pair_recv, out_send, out_recv, ring_send, ring_recv):
     cells, y = lax.axis_index("cells"), lax.axis_index("holes")
@@ -117,19 +117,20 @@
 
     for copy in ins + small:
         copy.wait()
+    bas_own[...] = jnp.transpose(bas[y].astype(F32)).astype(BF16)
     far = []
-    for n, axis in enumerate("xz"):
+    for n, axis in enumerate("yxz"):
+        bas_t[n, :, 0:LANES] = bas_own[...]
         for d in range(1, 4):
-            far.append(pltpu.make_async_remote_copy(src_ref=bas.at[y], dst_ref=bas_far.at[n, 4 - d], send_sem=bas_send.at[n, d], recv_sem=bas_recv.at[n, 4 - d],
-                                                    device_id=at(**{axis: d}), device_id_type=MESH))
+            if axis == "y":
+                bas_t[n, :, d * LANES:(d + 1) * LANES] = jnp.transpose(bas[on_ring(d)].astype(F32)).astype(BF16)
+                continue
+            far.append(pltpu.make_async_remote_copy(
+                src_ref=bas_own, dst_ref=bas_t.at[n, :, pl.ds((4 - d) * LANES, LANES)], send_sem=bas_send.at[n, d], recv_sem=bas_recv.at[n, 4 - d],
+                device_id=at(**{axis: d}), device_id_type=MESH))
             far[-1].start()
-    for copy in idx_copies + far:
+    for copy in idx_copies:
         copy.wait()
-    for d in range(4):
-        columns = slice(d * LANES, (d + 1) * LANES)
-        for n, axis in enumerate("yxz"):
-            piece = bas[on_ring(d)] if axis == "y" else bas[y] if d == 0 else bas_far[n - 1, d]
-            bas_t[n, :, columns] = jnp.transpose(piece.astype(F32)).astype(BF16)
     starts = [0]
     for g in range(NY - 1):
         starts.append(starts[-1] + live[g])
@@ -138,26 +139,20 @@
         lists[g * 16:(g + 1) * 16, :] = all_idx[first:first + 16, :] * ROW
     lane = lax.broadcasted_iota(I32, (LIST, LANES), 1)
     place = lax.broadcasted_iota(I32, (LIST, LANES), 0) * LANES + lane
-    for s, (axis, lo, hi) in enumerate(SUBS):
-        for d in range(4):
-            row = lo * NY * CORES + (lax.rem(where_am_i[axis] + d, 4) * CORES + core) * (hi - lo)
-            found = []
-            for n, offset in enumerate((16, 48)):
-                total = jnp.zeros((LIST, LANES), I32)
-                for g in range(NY):
-                    whole, shift = starts[g] // LANES, starts[g] % LANES
-                    window = MARGIN + g * IDX_ROWS + offset + jnp.clip(row - whole, -LIST, Q_ROWS)
-                    same = pltpu.roll(all_idx[pl.ds(window, LIST), :], shift, 1)
-                    before = pltpu.roll(all_idx[pl.ds(window - 1, LIST), :], shift, 1)
-                    values = jnp.where(lane >= shift, same, before)
-                    if n == 0:
-                        values = values + g * DIP_G
-                    since = place + (row * LANES - starts[g])
-                    total = jnp.where((since >= 0) & (since < live[g]), values, total)
-                found.append(total[0:4, :])
-            first = NY * 16 + (s * 4 + d) * LIST
-            lists[first:first + LIST, :] = jnp.concatenate(found, axis=0) * ROW
-    to_smem = pltpu.make_async_copy(lists, idx.at[pl.ds(0, lists.shape[0])], idx_sem)
+    for n, offset in enumerate((16, 48)):
+        total = jnp.zeros((LIST, LANES), I32)
+        for g in range(NY):
+            whole, shift = starts[g] // LANES, starts[g] % LANES
+            window = MARGIN + g * IDX_ROWS + offset - whole
+            same = pltpu.roll(all_idx[pl.ds(window, LIST), :], shift, 1)
+            before = pltpu.roll(all_idx[pl.ds(window - 1, LIST), :], shift, 1)
+            values = jnp.where(lane >= shift, same, before)
+            if n == 0:
+                values = values + g * DIP_G
+            since = place - starts[g]
+            total = jnp.where((since >= 0) & (since < live[g]), values, total)
+        lists[NY * 16 + n * LIST:NY * 16 + (n + 1) * LIST, :] = total * ROW
+    to_smem = pltpu.make_async_copy(lists, idx.at[pl.ds(0, lists.shape[0]), :], idx_sem)
     to_smem.start()
     to_smem.wait()
 
@@ -185,6 +180,13 @@
         spread(y, piece)
 
     forwards = []
+
+    def from_sibling(dy, n):
+        forward_there = landed.at[:, rows_of(on_ring(dy), n * CORES + 1 - core), :]
+        pltpu.make_async_remote_copy(src_ref=forward_there, dst_ref=forward_there, send_sem=fwd_send.at[dy, n], recv_sem=fwd_recv.at[dy, n],
+                                     device_id=sibling, device_id_type=MESH).wait_recv()
+        spread(on_ring(dy), n * CORES + 1 - core)
+
     for n in range(PARTS // CORES):
         for dy in (1, 3, 2):
             where = landed.at[:, rows_of(on_ring(dy), n * CORES + core), :]
@@ -193,15 +195,13 @@
             forwards.append(forward(dy, n))
             forwards[-1].start()
             spread(on_ring(dy), n * CORES + core)
-    for n in range(PARTS // CORES):
-        for dy in (1, 3, 2):
-            where = landed.at[:, rows_of(on_ring(dy), n * CORES + 1 - core), :]
-            pltpu.make_async_remote_copy(src_ref=where, dst_ref=where, send_sem=fwd_send.at[dy, n], recv_sem=fwd_recv.at[dy, n],
-                                         device_id=sibling, device_id_type=MESH).wait_recv()
-            spread(on_ring(dy), n * CORES + 1 - core)
+            if n:
+                from_sibling(dy, n - 1)
+    for dy in (1, 3, 2):
+        from_sibling(dy, PARTS // CORES - 1)
 
     def column(u, down):
-        return idx.at[pl.ds(down, idx.shape[0] - LIST), pl.ds(u, 1)]
+        return idx.at[pl.ds(down, idx.shape[0] - LIST - 2), pl.ds(u, 1)]
 
     def dipoles(b, _):
         for k in range(2):
@@ -218,10 +218,13 @@
     mine = wts[lax.rem(y, CORES), pl.ds(lax.div(y, CORES), 1), :]
 
     def candidates(s, d):
-        row = NY * 16 + (s * 4 + d) * LIST
+        there = jnp.int32(0)
+        for n, (axis, _, _) in enumerate(SUBS):
+            there = jnp.where(s == n, where_am_i[axis], there)
+        row = NY * 16 + s * 16 + (lax.rem(there + d, 4) * CORES + core) * 2
         for k in range(2):
             for u in range(BLOCK):
-                near, far = column(u, k)[row, 0], column(u, k + 4)[row, 0]
+                near, far = column(u, k)[row, 0], column(u, k + LIST)[row, 0]
                 spot = (k * BLOCK + u) * ROW
                 prod[spot:spot + ROW, :] = dtab[pl.ds(near, ROW), :] * dtab[pl.ds(far, ROW), :]
             one, two, three = (prod[pl.ds(k * BLOCK * ROW + c, BLOCK, stride=ROW), :] for c in range(3))
@@ -338,6 +341,8 @@
                 project(s)
         return 0
 
+    for copy in far:
+        copy.wait()
     lax.fori_loop(0, 4 * len(SUBS), steps, 0)
     for s in range(len(SUBS) - LAG, len(SUBS)):
         project(s)
@@ -346,6 +351,18 @@
         add_up(s)
         if s - 1 in hopping:
             send_out(s - 1)
+    for s in range(len(SUBS)):
+        for d in range(1, 4):
+            sens_copy(s, d).wait_send()
+        for d in range(len(deltas)):
+            part_copy(s, d).wait_send()
+    for copy in forwards:
+        copy.wait_send()
+    for h in range(2):
+        @pl.when(h * CORES + core != y)
+        def _():
+            for piece in range(PARTS):
+                pole_copy(h, piece).wait_send()
     for s, (axis, lo, hi) in enumerate(SUBS):
         if s not in hopping:
             for dc, dy in ring:
@@ -375,11 +392,7 @@
         turned = then
 
     for s in range(len(SUBS)):
-        for d in range(1, 4):
-            sens_copy(s, d).wait_send()
-        for d in range(len(deltas)):
-            part_copy(s, d).wait_send()
-        if SUBS[s][0] == "y":
+        if s not in hopping:
             for dc, dy in ring:
                 ring_copy(s, dc, dy).wait_send()
             continue
@@ -390,13 +403,6 @@
         @pl.when(share(s) != chip)
         def _():
             out_copy(s, 0, 0).wait_send()
-    for copy in forwards:
-        copy.wait_send()
-    for h in range(2):
-        @pl.when(h * CORES + core != y)
-        def _():
-            for piece in range(PARTS):
-                pole_copy(h, piece).wait_send()
 
 
 def on_device(pole_grads, endpoints, current, potential, live_counts, cell_weight, basis):
@@ -415,14 +421,14 @@
             vmem((NY * POLES_G * ROW, LANES), F32),
             vmem((NY * DIP_G * ROW, LANES), F32),
             vmem((MARGIN + NY * IDX_ROWS + MARGIN, LANES), I32),
-            vmem((NY * 16 + len(SUBS) * 4 * LIST, LANES), I32),
-            pltpu.SMEM((NY * 16 + len(SUBS) * 4 * LIST + LIST, LANES), I32),
+            vmem((NY * 16 + 2 * LIST, LANES), I32),
+            pltpu.SMEM((NY * 16 + 2 * LIST + 2, LANES), I32),
             vmem((2 * BLOCK * ROW, LANES), F32),
             vmem((NY, OWN_Q, LANES), BF16),
             vmem((NY, OWN_Q, LANES), BF16),
             vmem((CORES, 2, LANES), F32),
             vmem((NY, LANES, BASIS), BF16),
-            vmem((2, 4, LANES, BASIS), BF16),
+            vmem((BASIS, LANES), BF16),
             vmem((3, BASIS, 4 * LANES), BF16),
             vmem((CHIPS, BASIS // CHIPS, OWN_Q), BF16),
             vmem((CHIPS - 1, BASIS // CHIPS, OWN_Q), BF16),
@@ -434,7 +440,7 @@
             dma((2, PARTS)), dma((NY, PARTS // CORES)), dma((NY, PARTS // CORES)), dma((NY, PARTS // CORES)), dma,
             dma((NY, 3)), dma((NY, 3)), dma,
             dma((3,)), dma((3,)),
-            dma((2, 4)), dma((2, 4)),
+            dma((3, 4)), dma((3, 4)),
             dma((len(SUBS), 4)), dma((len(SUBS), 4)),
             dma((len(SUBS), CHIPS - 1)), dma((len(SUBS), CHIPS - 1)),
             dma((len(SUBS),)), dma((len(SUBS),)),

time: 75.5 us -> 74.3 us (0.984)
  Pallas kernels: 73.8 us -> 72.6 us
    pallas_call x1, Pallas kernels: 73.8 us -> 72.6 us  [on_device(): pl.pallas_call(kernel, out_shape=jax.ShapeDtypeStruct((BASIS // CHIPS //...]
where the time goes in v4:
time: 74.3 us; the launch traced here: 74.2 us
  Pallas kernels  72.6 us (98%)
  other arithmetic  1.54 us (2%)
    pallas_call x1, Pallas kernels, on_device(): pl.pallas_call(kernel, out_shape=jax.ShapeDtypeStruct((BASIS // CHIPS //...  72.6 us
    convert_element_type x1, other arithmetic, on_device(): return gains.astype(BF16)  1.54 us

profile of v4, /device:TPU:1, one launch (start us, length us, event | category | flops | bytes accessed | tf_op | source)
XLA Modules:
  0.0 74.2 jit_solution(12977029687873126773)
XLA Ops:
  0.0 72.6 %shard_map.73 = f32[8,4096]{1,0:T(8,128)} custom-call(bf16[3,1536,256]{2,1,0:T(8,128)(2,1)} %bitcast.11, s32[16,128]{1,0:T(8,128)} %bitcast.14, s32[32,128]{1,0:T(8,128)} %bitcast.12, s32[32,128]{1,0:T(8,128)} %bitcast.13, s32[4]{0:T(128)} %live.1, f32[2,128]{1,0:T(2,128)} %bitcast.15, bf16[256,256]{1,0:T(8,128)(2,1)} %basis.1), custom_call_target="tpu_custom_call" | custom-call | tf_op jit(solution)/shard_map/pallas_call | solution.py:414
  72.6 1.5 %convert_element_type.3 = bf16[8,4096]{1,0:T(8,128)(2,1)} convert(f32[8,4096]{1,0:T(8,128)} %shard_map.73) | non-fusion elementwise | flops 32768 | bytes 196608 | tf_op jit(solution)/shard_map/convert_element_type | solution.py:452

commit v5 on v4

--- a/solution.py
+++ b/solution.py
@@ -22,7 +22,7 @@
 OWN_BLOCKS = LIVE // (NY * CORES * BLOCK)
 OWN_Q = OWN_BLOCKS * BLOCK
 SUBS = (("y", 0, 2), ("x", 2, 4), ("z", 4, 6), ("x", 6, 8), ("y", 8, 10))
-LAG = 3
+LAG = 4
 PLANE = {"y": ("x", "z"), "x": ("y", "z"), "z": ("x", "y")}
 IDX_ROWS = 80
 Q_ROWS = Q_G // LANES

time: 74.3 us -> 73.2 us (0.985)
  Pallas kernels: 72.6 us -> 71.6 us
    pallas_call x1, Pallas kernels: 72.6 us -> 71.6 us  [on_device(): pl.pallas_call(kernel, out_shape=jax.ShapeDtypeStruct((BASIS // CHIPS //...]
where the time goes in v5:
time: 73.2 us; the launch traced here: 73.1 us
  Pallas kernels  71.6 us (98%)
  other arithmetic  1.54 us (2%)
    pallas_call x1, Pallas kernels, on_device(): pl.pallas_call(kernel, out_shape=jax.ShapeDtypeStruct((BASIS // CHIPS //...  71.6 us
    convert_element_type x1, other arithmetic, on_device(): return gains.astype(BF16)  1.54 us

profile of v5, /device:TPU:1, one launch (start us, length us, event | category | flops | bytes accessed | tf_op | source)
XLA Modules:
  0.0 73.1 jit_solution(699578740399263947)
XLA Ops:
  0.0 71.6 %shard_map.73 = f32[8,4096]{1,0:T(8,128)} custom-call(bf16[3,1536,256]{2,1,0:T(8,128)(2,1)} %bitcast.11, s32[16,128]{1,0:T(8,128)} %bitcast.14, s32[32,128]{1,0:T(8,128)} %bitcast.12, s32[32,128]{1,0:T(8,128)} %bitcast.13, s32[4]{0:T(128)} %live.1, f32[2,128]{1,0:T(2,128)} %bitcast.15, bf16[256,256]{1,0:T(8,128)(2,1)} %basis.1), custom_call_target="tpu_custom_call" | custom-call | tf_op jit(solution)/shard_map/pallas_call | solution.py:414
  71.6 1.5 %convert_element_type.3 = bf16[8,4096]{1,0:T(8,128)(2,1)} convert(f32[8,4096]{1,0:T(8,128)} %shard_map.73) | non-fusion elementwise | flops 32768 | bytes 196608 | tf_op jit(solution)/shard_map/convert_element_type | solution.py:452

commit v6 on v5

--- a/solution.py
+++ b/solution.py
@@ -22,7 +22,7 @@
 OWN_BLOCKS = LIVE // (NY * CORES * BLOCK)
 OWN_Q = OWN_BLOCKS * BLOCK
 SUBS = (("y", 0, 2), ("x", 2, 4), ("z", 4, 6), ("x", 6, 8), ("y", 8, 10))
-LAG = 4
+LAG = 5
 PLANE = {"y": ("x", "z"), "x": ("y", "z"), "z": ("x", "y")}
 IDX_ROWS = 80
 Q_ROWS = Q_G // LANES

time: 73.2 us -> 73.2 us (level)
  no operation moved by 1% of the time
where the time goes in v6:
time: 73.2 us; the launch traced here: 73 us
  Pallas kernels  71.5 us (98%)
  other arithmetic  1.54 us (2%)
    pallas_call x1, Pallas kernels, on_device(): pl.pallas_call(kernel, out_shape=jax.ShapeDtypeStruct((BASIS // CHIPS //...  71.5 us
    convert_element_type x1, other arithmetic, on_device(): return gains.astype(BF16)  1.54 us

profile of v6, /device:TPU:1, one launch (start us, length us, event | category | flops | bytes accessed | tf_op | source)
XLA Modules:
  0.0 73.0 jit_solution(10650115602812845577)
XLA Ops:
  0.0 71.5 %shard_map.73 = f32[8,4096]{1,0:T(8,128)} custom-call(bf16[3,1536,256]{2,1,0:T(8,128)(2,1)} %bitcast.11, s32[16,128]{1,0:T(8,128)} %bitcast.14, s32[32,128]{1,0:T(8,128)} %bitcast.12, s32[32,128]{1,0:T(8,128)} %bitcast.13, s32[4]{0:T(128)} %live.1, f32[2,128]{1,0:T(2,128)} %bitcast.15, bf16[256,256]{1,0:T(8,128)(2,1)} %basis.1), custom_call_target="tpu_custom_call" | custom-call | tf_op jit(solution)/shard_map/pallas_call | solution.py:414
  71.5 1.5 %convert_element_type.3 = bf16[8,4096]{1,0:T(8,128)(2,1)} convert(f32[8,4096]{1,0:T(8,128)} %shard_map.73) | non-fusion elementwise | flops 32768 | bytes 196608 | tf_op jit(solution)/shard_map/convert_element_type | solution.py:452
